TPU v7x, 32 devices: a whole 2x2x4 slice. The times are simulated.
32 devices in a mesh: section: 2 (over y), seq: 4 (over z), chan: 4 (over x, core).
Axes of the slice: x: 2, y: 2, z: 4, core: 2. Of those that a mesh axis runs over, the one named last changes fastest.
Arguments:
- layer_rows: bfloat16 [2, 4096, 8192], P('section', 'seq', 'chan'), may hold values from -6 to 6
- in_weight: bfloat16 [2, 8192, 768], P('section', 'chan'), may hold values from -0.0625 to 0.0625
- long_filter: float32 [2, 4096, 256], P('section', ('seq', 'chan')), may hold values from -2 to 2, as said below
- skip_gain: float32 [2, 256], P('section'), may hold values from -4 to 4
Outputs:
- gated_out: bfloat16 [2, 4096, 256], P('section', ('seq', 'chan'))
Inputs may be any that keep to these rules, and one draw needn't show every extreme that they name: `long_filter`: filter taps of each channel.
All inputs are finite; a program needn't handle non-finite values.
Results may differ from a plain program's by a relative error of at most 0.0064.
Values may be sent and summed in bfloat16 or wider, within the bound.
A program may use at most 64 MiB of HBM per device.

v0:
```python
import math

import jax
import jax.numpy as jnp
from jax import lax
from jax.sharding import PartitionSpec as P


def from_behind(value, axis, steps):
    count = lax.axis_size(axis)
    pairs = [(source, (source + steps) % count) for source in range(count)]
    return lax.ppermute(value, axis, pairs)


def transpose_blocks(data):
    return lax.all_to_all(data, ("seq", "chan"), split_axis=0, concat_axis=1, tiled=True)


def mix(table, data, form):
    return jnp.einsum(form, table, data, precision=lax.Precision.HIGHEST)


def body(layer_rows, in_weight, long_filter, skip_gain):
    chan_width = long_filter.shape[2]
    row_count = long_filter.shape[1]
    seq_devices = lax.axis_size(("seq", "chan"))
    block_rows = row_count // seq_devices
    fft_length = 2 * row_count * seq_devices
    device_index = lax.axis_index(("seq", "chan"))
    source = from_behind(layer_rows, "section", 1)
    picked = source[0]
    summed = lax.psum_scatter(
        jnp.dot(picked, in_weight[0], preferred_element_type=jnp.float32),
        "chan",
        scatter_dimension=0,
        tiled=True,
    )
    mixed = summed.astype(jnp.bfloat16)
    queries = mixed[:, :chan_width].astype(jnp.float32)
    key_part = mixed[:, chan_width : 2 * chan_width].astype(jnp.float32)
    values_part = mixed[:, 2 * chan_width :].astype(jnp.float32)
    signal = key_part * values_part
    coarse_freq = jnp.arange(2 * seq_devices, dtype=jnp.int32)
    block_ids = jnp.arange(seq_devices, dtype=jnp.int32)
    coarse_angle = (
        2.0
        * math.pi
        / (2 * seq_devices)
        * (coarse_freq[:, None] * block_ids[None, :] % (2 * seq_devices)).astype(jnp.float32)
    )
    coarse_cos = jnp.cos(coarse_angle)
    coarse_sin = jnp.sin(coarse_angle)
    positions = device_index * block_rows + jnp.arange(block_rows, dtype=jnp.int32)
    twist_angle = (
        2.0
        * math.pi
        / fft_length
        * (coarse_freq[:, None] * positions[None, :] % fft_length).astype(jnp.float32)
    )
    twist_cos = jnp.cos(twist_angle)[:, :, None]
    twist_sin = jnp.sin(twist_angle)[:, :, None]
    fine_ids = jnp.arange(row_count, dtype=jnp.int32)
    fine_angle = (
        2.0
        * math.pi
        / row_count
        * (fine_ids[:, None] * fine_ids[None, :] % row_count).astype(jnp.float32)
    )
    fine_cos = jnp.cos(fine_angle)
    fine_sin = jnp.sin(fine_angle)
    paired = jnp.concatenate([signal, long_filter[0]], axis=1)
    blocks = transpose_blocks(paired.reshape(seq_devices, 1, block_rows, 2 * chan_width))
    blocks = blocks.reshape(seq_devices, block_rows, 2 * chan_width)
    coarse_real = mix(coarse_cos, blocks, "km,mrc->krc")
    coarse_imag = -mix(coarse_sin, blocks, "km,mrc->krc")
    twist_real = coarse_real * twist_cos + coarse_imag * twist_sin
    twist_imag = coarse_imag * twist_cos - coarse_real * twist_sin
    packed = jnp.concatenate([twist_real, twist_imag], axis=2)
    arrived = transpose_blocks(packed.reshape(2 * seq_devices, 1, block_rows, 4 * chan_width))
    arrived = arrived.reshape(2, row_count, 4 * chan_width)
    inner_real = arrived[:, :, : 2 * chan_width]
    inner_imag = arrived[:, :, 2 * chan_width :]
    spec_real = mix(fine_cos, inner_real, "kr,jrc->jkc") + mix(fine_sin, inner_imag, "kr,jrc->jkc")
    spec_imag = mix(fine_cos, inner_imag, "kr,jrc->jkc") - mix(fine_sin, inner_real, "kr,jrc->jkc")
    sig_real = spec_real[:, :, :chan_width]
    sig_imag = spec_imag[:, :, :chan_width]
    fil_real = spec_real[:, :, chan_width:]
    fil_imag = spec_imag[:, :, chan_width:]
    prod_real = sig_real * fil_real - sig_imag * fil_imag
    prod_imag = sig_real * fil_imag + sig_imag * fil_real
    fine_cos3 = fine_cos.reshape(seq_devices, block_rows, row_count)
    fine_sin3 = fine_sin.reshape(seq_devices, block_rows, row_count)
    back_real = mix(fine_cos3, prod_real, "qpk,jkc->qjpc") - mix(
        fine_sin3, prod_imag, "qpk,jkc->qjpc"
    )
    back_imag = mix(fine_cos3, prod_imag, "qpk,jkc->qjpc") + mix(
        fine_sin3, prod_real, "qpk,jkc->qjpc"
    )
    returned = transpose_blocks(jnp.concatenate([back_real, back_imag], axis=3))
    returned = returned.reshape(2 * seq_devices, block_rows, 2 * chan_width)
    ret_real = returned[:, :, :chan_width]
    ret_imag = returned[:, :, chan_width:]
    untwist_real = ret_real * twist_cos - ret_imag * twist_sin
    untwist_imag = ret_imag * twist_cos + ret_real * twist_sin
    conv_blocks = (
        mix(coarse_cos, untwist_real, "km,krc->mrc") - mix(coarse_sin, untwist_imag, "km,krc->mrc")
    ) / fft_length
    conv = transpose_blocks(conv_blocks.reshape(seq_devices, 1, block_rows, chan_width))
    conv = conv.reshape(row_count, chan_width)
    gated_out = queries * (conv + skip_gain[0][None, :] * signal)
    return gated_out.astype(jnp.bfloat16)[None]


def solution(mesh):
    in_specs = (
        P("section", "seq", "chan"),
        P("section", "chan", None),
        P("section", ("seq", "chan"), None),
        P("section", None),
    )
    out_specs = P("section", ("seq", "chan"), None)
    return jax.shard_map(body, mesh=mesh, in_specs=in_specs, out_specs=out_specs, check_vma=False)
```

profile of v0, /device:TPU:0, one launch (start us, length us, event | category | flops | bytes accessed | tf_op | source)
XLA Modules:
  0.0 302.2 jit_solution(14423697191729224871)
XLA Ops:
  6.5 3.0 collective-permute-start
  9.5 90.8 %collective-permute-done = bf16[1,1024,2048]{2,1,0:T(8,128)(2,1)S(1)} collective-permute-done((bf16[1,1024,2048]{2,1,0:T(8,128)(2,1)}, bf16[1,1024,2048]{2,1,0:T(8,128)(2,1)S(1)}, u32[]{:S(2)}, u32[]{:S(2)}) %collective-permute-start) | collective-permute-done | bytes 4194336 | tf_op jit(solution)/shard_map/ppermute | solution.py:12
  100.3 5.1 %fusion = f32[1024,768]{1,0:T(8,128)} fusion(bf16[1,1024,2048]{2,1,0:T(8,128)(2,1)S(1)} %collective-permute-done, bf16[1,2048,768]{2,1,0:T(8,128)(2,1)S(1)} %copy-done), kind=kOutput, calls=%fused_computation | convolution fusion | flops 3221225472 | bytes 10485760 | tf_op jit(solution)/shard_map/dot_general | solution.py:33
  105.4 39.6 %reduce-scatter.2.cloned.1.call-done = f32[256,768]{1,0:T(8,128)} async-done(((f32[1024,768]{1,0:T(8,128)}), f32[256,768]{1,0:T(8,128)}) %reduce-scatter.2.cloned.1.call-update) | async-done | bytes 786448 | tf_op jit(solution)/shard_map/reduce_scatter | solution.py:32
  145.0 1.2 convert_element_type.53
  146.2 1.8 maximum_bitcast_fusion.1
  148.0 4.8 %all-to-all-start = ((f32[16,1,16,512]{3,2,1,0:T(8,128)}), f32[16,1,16,512]{3,2,1,0:T(8,128)}, u32[]{:S(2)}, u32[]{:S(2)}) async-start(f32[16,1,16,512]{3,2,1,0:T(8,128)} %maximum_bitcast_fusion.1), calls=%async_computation.1 | async-start | bytes 1048576 | tf_op jit(solution)/shard_map/all_to_all | solution.py:16
  152.9 14.4 %all-to-all-done = f32[16,1,16,512]{3,2,1,0:T(8,128)} async-done(((f32[16,1,16,512]{3,2,1,0:T(8,128)}), f32[16,1,16,512]{3,2,1,0:T(8,128)}, u32[]{:S(2)}, u32[]{:S(2)}) %all-to-all-start) | async-done | bytes 524320 | tf_op jit(solution)/shard_map/all_to_all | solution.py:16
  167.3 2.2 fusion.22
  169.5 2.5 multiply_add_fusion
  172.2 2.5 copy.44
  174.7 4.6 %all-to-all-start.1 = ((f32[32,1,16,1024]{3,2,1,0:T(8,128)}), f32[32,1,16,1024]{3,2,1,0:T(8,128)}, u32[]{:S(2)}, u32[]{:S(2)}) async-start(f32[32,1,16,1024]{3,2,1,0:T(8,128)} %copy.44), calls=%async_computation.2 | async-start | bytes 4194304 | tf_op jit(solution)/shard_map/all_to_all | solution.py:16
  179.4 40.9 %all-to-all-done.1 = f32[32,1,16,1024]{3,2,1,0:T(8,128)} async-done(((f32[32,1,16,1024]{3,2,1,0:T(8,128)}), f32[32,1,16,1024]{3,2,1,0:T(8,128)}, u32[]{:S(2)}, u32[]{:S(2)}) %all-to-all-start.1) | async-done | bytes 2097184 | tf_op jit(solution)/shard_map/all_to_all | solution.py:16
  220.2 1.7 copy.45
  222.0 2.7 fusion.10
  224.6 2.7 fusion.12
  227.3 2.7 fusion.3
  230.0 2.7 fusion.4
  232.8 1.8 fusion.18
  234.6 1.6 fusion.16
  236.2 1.6 fusion.5
  237.8 1.6 fusion.6
  239.6 1.1 copy.52
  240.7 11.2 %all-to-all-start.2 = ((f32[16,2,16,512]{3,2,1,0:T(8,128)}), f32[16,2,16,512]{3,2,1,0:T(8,128)}, u32[]{:S(2)}, u32[]{:S(2)}) async-start(f32[16,2,16,512]{3,2,1,0:T(8,128)} %copy.52), calls=%async_computation.3 | async-start | bytes 2097152 | tf_op jit(solution)/shard_map/all_to_all | solution.py:16
  251.9 0.7 copy.54
  252.6 0.7 copy.53
  253.3 21.6 %all-to-all-done.2 = f32[16,2,16,512]{3,2,1,0:T(8,128)} async-done(((f32[16,2,16,512]{3,2,1,0:T(8,128)}), f32[16,2,16,512]{3,2,1,0:T(8,128)}, u32[]{:S(2)}, u32[]{:S(2)}) %all-to-all-start.2) | async-done | bytes 1048608 | tf_op jit(solution)/shard_map/all_to_all | solution.py:16
  274.9 1.4 multiply_add_fusion.1
  276.3 0.7 fusion.25
  277.0 0.7 fusion.8
  277.9 16.7 %all_to_all.42 = f32[16,1,16,256]{3,2,1,0:T(8,128)S(1)} all-to-all(f32[16,1,16,256]{3,2,1,0:T(8,128)S(1)} %copy.57), channel_id=1, replica_groups=mesh['section'=2,'seq'=4,'chan'=4] {'seq','chan'}, dimensions={0} | all-to-all | bytes 524288 | tf_op jit(solution)/shard_map/all_to_all | solution.py:16
  294.6 0.7 fusion.36
  (18 shorter events, 0.8 us)
Async XLA Ops:
  6.5 93.8 %copy-start = (bf16[1,2048,768]{2,1,0:T(8,128)(2,1)S(1)}, bf16[1,2048,768]{2,1,0:T(8,128)(2,1)}, u32[]{:S(2)}) copy-start(bf16[1,2048,768]{2,1,0:T(8,128)(2,1)} %param.5) | copy-start | bytes 9437188
  6.5 138.4 %reduce-scatter.2.cloned.1.call-start = ((), (), s32[]{:S(2)}) async-start(), calls=%async_computation.5 | async-start | bytes 3932160 | tf_op jit(solution)/shard_map/reduce_scatter | solution.py:32
  6.5 93.7 %collective-permute-start = (bf16[1,1024,2048]{2,1,0:T(8,128)(2,1)}, bf16[1,1024,2048]{2,1,0:T(8,128)(2,1)S(1)}, u32[]{:S(2)}, u32[]{:S(2)}) collective-permute-start(bf16[1,1024,2048]{2,1,0:T(8,128)(2,1)} %param.4), channel_id=1, source_target_pairs={{0,16},{16,0},{1,17},{17,1},{2,18},{18,2},{3,19},{19,3},{4,20},{20... | collective-permute-start | bytes 12582920 | tf_op jit(solution)/shard_map/ppermute | solution.py:12
  148.0 19.3 %all-to-all-start = ((f32[16,1,16,512]{3,2,1,0:T(8,128)}), f32[16,1,16,512]{3,2,1,0:T(8,128)}, u32[]{:S(2)}, u32[]{:S(2)}) async-start(f32[16,1,16,512]{3,2,1,0:T(8,128)} %maximum_bitcast_fusion.1), calls=%async_computation.1 | async-start | bytes 1048576 | tf_op jit(solution)/shard_map/all_to_all | solution.py:16
  152.9 19.1 %copy-start.1 = (f32[32,16]{0,1:T(8,128)}, f32[32,16]{0,1:T(8,128)S(1)}, u32[]{:S(2)}) copy-start(f32[32,16]{0,1:T(8,128)S(1)} %get-tuple-element.12) | copy-start | bytes 6148
  174.7 45.5 %all-to-all-start.1 = ((f32[32,1,16,1024]{3,2,1,0:T(8,128)}), f32[32,1,16,1024]{3,2,1,0:T(8,128)}, u32[]{:S(2)}, u32[]{:S(2)}) async-start(f32[32,1,16,1024]{3,2,1,0:T(8,128)} %copy.44), calls=%async_computation.2 | async-start | bytes 4194304 | tf_op jit(solution)/shard_map/all_to_all | solution.py:16
  239.6 12.3 %copy-start.2 = (f32[32,16]{0,1:T(8,128)S(1)}, f32[32,16]{0,1:T(8,128)}, u32[]{:S(2)}) copy-start(f32[32,16]{0,1:T(8,128)} %copy-done.1) | copy-start | bytes 6148
  240.7 34.2 %all-to-all-start.2 = ((f32[16,2,16,512]{3,2,1,0:T(8,128)}), f32[16,2,16,512]{3,2,1,0:T(8,128)}, u32[]{:S(2)}, u32[]{:S(2)}) async-start(f32[16,2,16,512]{3,2,1,0:T(8,128)} %copy.52), calls=%async_computation.3 | async-start | bytes 2097152 | tf_op jit(solution)/shard_map/all_to_all | solution.py:16
  274.9 19.7 %copy-start.3 = (f32[1,256]{1,0:T(1,128)S(1)}, f32[1,256]{1,0:T(1,128)}, u32[]{:S(2)}) copy-start(f32[1,256]{1,0:T(1,128)} %param.7) | copy-start | bytes 3076
Sparse Core Ops, SparseCore 0:
  105.5 39.4 reduce-scatter.1
where the time goes:
time: 303 us; the launch traced here: 302 us
  waiting for transfers between devices  207 us (68%)
  matrix products  28.4 us (9%)
  starting transfers between devices  23.6 us (8%)
  blocking collectives  16.7 us (6%)
  between operations  13.6 us (4%)
  local copies, waits for them, and re-layouts  6.86 us (2%)
  other arithmetic  5.74 us (2%)
    ppermute x1, waiting for transfers between devices, from_behind(): return lax.ppermute(value, axis, pairs)  90.8 us
    all_to_all x3, waiting for transfers between devices, transpose_blocks(): lax.all_to_all(data, ('seq', 'chan'), split_axis=0, concat_axis=1, tiled=...  76.9 us
    reduce_scatter x1, waiting for transfers between devices, body(): lax.psum_scatter(jnp.dot(picked, in_weight[0], preferred_element_type=jnp...  39.6 us
    dot_general x12, matrix products, mix(): return jnp.einsum(form, table, data, precision=lax.Precision.HIGHEST)  23.3 us
    all_to_all x3, starting transfers between devices, transpose_blocks(): lax.all_to_all(data, ('seq', 'chan'), split_axis=0, concat_axis=1, tiled=...  20.6 us
    all_to_all x1, blocking collectives, transpose_blocks(): lax.all_to_all(data, ('seq', 'chan'), split_axis=0, concat_axis=1, tiled=...  16.7 us
  transfers between devices with their start and end apart: 5, of which 5 were waited for; matrix products, arithmetic and copies ran while one was open for 0% of the time, Pallas kernels for 0%

commit v1 on v0

v1 whole, which is shorter than its diff:
```python
import functools
import math

import jax
import jax.numpy as jnp
import numpy as np
from jax import lax
from jax.experimental import pallas as pl
from jax.experimental.pallas import tpu as pltpu
from jax.sharding import PartitionSpec as P

LANES = 128
PIECES = 2
MESH = pl.DeviceIdType.MESH
F32 = jnp.float32


def tables(positions):
    length = 2 * positions
    n1 = positions // LANES
    full = 2 * n1
    kept = n1 + 1
    rows = -(-kept // 8) * 8
    k1 = np.arange(kept)
    angle = 2 * math.pi * ((k1[:, None] * np.arange(n1)[None, :]) % full) / full
    first = np.zeros((2 * rows, n1), np.float32)
    first[:kept] = np.cos(angle)
    first[rows : rows + kept] = -np.sin(angle)
    weight = np.where((k1 == 0) | (k1 == n1), 1.0, 2.0) / length
    last = np.zeros((n1, 2 * rows), np.float32)
    last[:, :kept] = (np.cos(angle) * weight[:, None]).T
    last[:, rows : rows + kept] = -(np.sin(angle) * weight[:, None]).T
    n2 = np.arange(LANES)
    turn = 2 * math.pi * ((np.arange(rows)[:, None] * n2[None, :]) % length) / length
    twist = np.stack([np.cos(turn), np.sin(turn)]).astype(np.float32)
    fine = 2 * math.pi * ((n2[:, None] * n2[None, :]) % LANES) / LANES
    cos, sin = np.cos(fine), np.sin(fine)
    forward = np.block([[cos, -sin], [sin, cos]]).astype(np.float32)
    back = np.block([[cos, sin], [-sin, cos]]).astype(np.float32)
    return first, twist, forward, back, last


def exact(a, b):
    return jnp.dot(a, b, precision=lax.Precision.HIGHEST, preferred_element_type=F32)


def kernel(
    sizes,
    rows_hbm, weight_hbm, filter_hbm, first_ref, twist_ref, forward_ref, back_ref, last_ref,
    out_ref,
    rows_v, wbuf, part, held, fil_in, sig_out, sig_in, query, conv_out, conv_in, gate_out, gate_in,
    fil_line, line, spec_in, fil_spec,
    y_send, y_recv, z_send, z_recv, r_send, r_recv, f_send, f_recv,
    a_send, a_recv, b_send, b_recv, o_send, o_recv, local_sem,
):
    n_sec, n_seq, n_chan, group, share, tile_rows, k_rows = sizes
    sec, z, c = lax.axis_index("section"), lax.axis_index("seq"), lax.axis_index("chan")
    ahead = lax.rem(sec + 1, n_sec)
    behind = lax.rem(sec + n_sec - 1, n_sec)
    half = lax.rem(z, 2)
    mate = z + 1 - 2 * half
    c1 = c + 1 - 2 * lax.rem(c, 2)
    c2 = lax.rem(c + 2, 4)
    c3 = 3 - c
    order = (c3, c2, c1, c)

    def place(s, seq, chan):
        return (s, seq, chan)

    rows_copy = pltpu.make_async_copy(rows_hbm, rows_v, local_sem.at[0])
    rows_copy.start()

    barrier = pltpu.get_barrier_semaphore()

    def greet(i, carry):
        pl.semaphore_signal(
            barrier, inc=1, device_id=place(ahead, i // n_chan, i % n_chan), device_id_type=MESH
        )
        return carry

    lax.fori_loop(0, n_seq * n_chan, greet, 0)
    for other in range(n_chan):
        pl.semaphore_signal(barrier, inc=1, device_id=place(behind, z, other), device_id_type=MESH)
    pl.semaphore_signal(barrier, inc=1, device_id=place(sec, z, c1), device_id_type=MESH)
    pl.semaphore_signal(barrier, inc=1, device_id=place(sec, z, c2), device_id_type=MESH)
    for step in range(1, n_seq):
        pl.semaphore_signal(
            barrier, inc=1, device_id=place(sec, lax.rem(z + step, n_seq), c), device_id_type=MESH
        )
    pl.semaphore_wait(barrier, n_seq * n_chan + n_chan + 2 + n_seq - 1)

    def remote(src, dst, send, recv, target):
        return pltpu.make_async_remote_copy(
            src_ref=src, dst_ref=dst, send_sem=send, recv_sem=recv, device_id=target,
            device_id_type=MESH,
        )

    me = z * n_chan + c

    def filter_copy(i):
        seq, chan = i // n_chan, i % n_chan
        return remote(
            filter_hbm.at[chan * n_seq + seq], fil_in.at[me], f_send.at[i], f_recv.at[me],
            place(behind, seq, chan),
        )

    def filter_wait(i):
        return remote(
            filter_hbm.at[0], fil_in.at[i], f_send.at[i], f_recv.at[i], place(behind, z, c)
        )

    def start_filter(i, carry):
        filter_copy(i).start()
        return carry

    def end_filter(i, carry):
        filter_copy(i).wait_send()
        filter_wait(i).wait_recv()
        return carry

    total = 4 * PIECES

    def piece(k, which):
        return order[k // PIECES] * (2 * PIECES) + which * PIECES + k % PIECES

    def over_y(k):
        at = piece(k, half)
        return remote(
            weight_hbm.at[at], wbuf.at[at], y_send.at[k], y_recv.at[k], place(behind, z, c)
        )

    def over_z(k):
        at = piece(k, half)
        return remote(wbuf.at[at], wbuf.at[at], z_send.at[k], z_recv.at[k], place(sec, mate, c))

    def from_z(k):
        at = piece(k, 1 - half)
        return remote(wbuf.at[at], wbuf.at[at], z_send.at[k], z_recv.at[k], place(sec, mate, c))

    positions = rows_v.shape[0]
    columns = 3 * group
    pos_tile = 256

    def multiply(j, slot):
        block = wbuf[pl.ds(order[j] * 2 * PIECES, 2 * PIECES)].reshape(columns, rows_v.shape[1])

        def tile(t, carry):
            at = pl.multiple_of(t * pos_tile, pos_tile)
            part[slot, :, pl.ds(at, pos_tile)] = lax.dot_general(
                block, rows_v[pl.ds(at, pos_tile), :], (((1,), (1,)), ((), ())),
                preferred_element_type=F32,
            )
            return carry

        lax.fori_loop(0, positions // pos_tile, tile, 0)

    to_pair = remote(part.at[0], held.at[0], r_send.at[0], r_recv.at[0], place(sec, z, c1))
    to_cross = remote(part.at[1], held.at[1], r_send.at[1], r_recv.at[1], place(sec, z, c2))
    to_pair_last = remote(part.at[2], held.at[2], r_send.at[2], r_recv.at[2], place(sec, z, c1))

    def spectrum(source, target):
        mixed = exact(first_ref[...], source[...])
        for a in range(share):
            lanes = slice(a * LANES, (a + 1) * LANES)
            real, imag = mixed[:k_rows, lanes], mixed[k_rows:, lanes]
            span = slice(a * k_rows, (a + 1) * k_rows)
            spec_in[span, :LANES] = real * twist_ref[0] + imag * twist_ref[1]
            spec_in[span, LANES:] = imag * twist_ref[0] - real * twist_ref[1]
        target[...] = exact(spec_in[...], forward_ref[...])

    def process(j):
        for k in range(j * PIECES, (j + 1) * PIECES):
            from_z(k).wait_recv()
        multiply(j, j)
        if j == 0:
            to_pair.start()
        if j == 1:
            to_pair.wait_recv()
            part[1] = part[1] + held[0]
            to_cross.start()
        if j == 2:
            to_pair_last.start()

    over_y(0).start()
    over_y(1).start()
    lax.fori_loop(0, n_seq * n_chan, start_filter, 0)
    rows_copy.wait()
    for k in range(total):
        over_y(k).wait_recv()
        over_z(k).start()
        over_y(k).wait_send()
        if k + 2 < total:
            over_y(k + 2).start()
        if k == PIECES:
            lax.fori_loop(0, n_seq * n_chan, end_filter, 0)
            per = fil_in.shape[2] // LANES
            for i in range(n_seq * n_chan):
                for r in range(per):
                    for a in range(share):
                        fil_line[i * per + r : i * per + r + 1, a * LANES : (a + 1) * LANES] = (
                            fil_in[i, a : a + 1, r * LANES : (r + 1) * LANES]
                        )
            spectrum(fil_line, fil_spec)
        if k % PIECES == PIECES - 1 and k >= PIECES:
            process(k // PIECES - 1)
    process(3)
    to_pair_last.wait_recv()
    to_cross.wait_recv()
    mixed = (part[3] + held[2] + held[1]).astype(jnp.bfloat16).astype(F32)
    signal = mixed[group : 2 * group] * mixed[2 * group :]
    for r in range(tile_rows):
        lanes = slice(r * LANES, (r + 1) * LANES)
        sig_out[:, r, :] = signal[:, lanes]
        query[:, r, :] = mixed[:group, lanes]

    def sig_copy(step):
        to = lax.rem(z + step, n_seq)
        return remote(
            sig_out.at[pl.ds(to * share, share)], sig_in.at[z], a_send.at[step], a_recv.at[step],
            place(sec, to, c),
        )

    def sig_wait(step):
        source = lax.rem(z + n_seq - step, n_seq)
        return remote(
            sig_out.at[pl.ds(0, share)], sig_in.at[source], a_send.at[step], a_recv.at[step],
            place(sec, source, c),
        )

    for step in range(1, n_seq):
        sig_copy(step).start()
    sig_in[z] = sig_out[pl.ds(z * share, share)]
    for step in range(1, n_seq):
        sig_wait(step).wait_recv()

    for a in range(share):
        line[:, a * LANES : (a + 1) * LANES] = sig_in[:, a].reshape(n_seq * tile_rows, LANES)
    mixed_first = exact(first_ref[...], line[...])
    for a in range(share):
        lanes = slice(a * LANES, (a + 1) * LANES)
        real, imag = mixed_first[:k_rows, lanes], mixed_first[k_rows:, lanes]
        span = slice(a * k_rows, (a + 1) * k_rows)
        spec_in[span, :LANES] = real * twist_ref[0] + imag * twist_ref[1]
        spec_in[span, LANES:] = imag * twist_ref[0] - real * twist_ref[1]
    spec = exact(spec_in[...], forward_ref[...])
    sr, si = spec[:, :LANES], spec[:, LANES:]
    fr, fi = fil_spec[:, :LANES], fil_spec[:, LANES:]
    spec_in[:, :LANES] = sr * fr - si * fi
    spec_in[:, LANES:] = sr * fi + si * fr
    inner = exact(spec_in[...], back_ref[...])
    turned = []
    for a in range(share):
        span = slice(a * k_rows, (a + 1) * k_rows)
        real, imag = inner[span, :LANES], inner[span, LANES:]
        turned.append(
            jnp.concatenate(
                [
                    real * twist_ref[0] - imag * twist_ref[1],
                    imag * twist_ref[0] + real * twist_ref[1],
                ],
                axis=0,
            )
        )
    conv = exact(last_ref[...], jnp.concatenate(turned, axis=1))
    for a in range(share):
        conv_out[:, a] = conv[:, a * LANES : (a + 1) * LANES].reshape(n_seq, tile_rows, LANES)

    def conv_copy(step):
        to = lax.rem(z + step, n_seq)
        return remote(
            conv_out.at[to], conv_in.at[z], b_send.at[step], b_recv.at[step], place(sec, to, c)
        )

    def conv_wait(step):
        source = lax.rem(z + n_seq - step, n_seq)
        return remote(
            conv_out.at[0], conv_in.at[source], b_send.at[step], b_recv.at[step],
            place(sec, source, c),
        )

    for step in range(1, n_seq):
        conv_copy(step).start()
    conv_in[z] = conv_out[z]
    for step in range(1, n_seq):
        conv_wait(step).wait_recv()

    per = tile_rows // n_chan
    for r in range(tile_rows):
        gated = query[:, r, :] * conv_in[:, :, r, :].reshape(group, LANES)
        gate_out[r // per, :, (r % per) * LANES : (r % per + 1) * LANES] = gated.astype(
            jnp.bfloat16
        )

    def gate_copy(to):
        return remote(
            gate_out.at[to], gate_in.at[c], o_send.at[to], o_recv.at[c], place(ahead, z, to)
        )

    def gate_wait(source):
        return remote(
            gate_out.at[0], gate_in.at[source], o_send.at[source], o_recv.at[source],
            place(ahead, z, source),
        )

    for to in range(n_chan):
        gate_copy(to).start()
    for source in range(n_chan):
        gate_wait(source).wait_recv()
    whole = gate_in[...].astype(F32).reshape(n_chan * group, per * LANES)
    out_ref[...] = whole.T.astype(jnp.bfloat16)

    for k in range(total):
        over_z(k).wait_send()
    to_pair.wait_send()
    to_cross.wait_send()
    to_pair_last.wait_send()
    for step in range(1, n_seq):
        sig_copy(step).wait_send()
        conv_copy(step).wait_send()
    for to in range(n_chan):
        gate_copy(to).wait_send()


def body(n_sec, n_seq, n_chan, layer_rows, in_weight, long_filter, skip_gain):
    chan_width = long_filter.shape[2]
    block = long_filter.shape[1]
    positions, features = layer_rows.shape[1:]
    group = chan_width // n_chan
    share = group // n_seq
    tile_rows = positions // LANES
    n1 = n_seq * tile_rows
    first, twist, forward, back, last = tables(n_seq * positions)
    k_rows = twist.shape[1]
    weight = in_weight[0].reshape(features, 3, n_chan, group).transpose(2, 1, 3, 0)
    width = 3 * group // (2 * PIECES)
    weight = weight.reshape(n_chan * 2 * PIECES, width, features)
    at_start = lax.axis_index(("seq", "chan")) == 0
    tap = jnp.where(at_start, skip_gain[0], 0.0)
    taps = jnp.concatenate([long_filter[0, :1] + tap[None, :], long_filter[0, 1:]], axis=0)
    taps = taps.T.reshape(n_chan * n_seq, share, block)
    sizes = (n_sec, n_seq, n_chan, group, share, tile_rows, k_rows)
    vmem = pl.BlockSpec(memory_space=pltpu.VMEM)
    hbm = pl.BlockSpec(memory_space=pl.ANY)
    dma = pltpu.SemaphoreType.DMA
    devices = n_seq * n_chan
    total = 4 * PIECES
    scratch = [
        pltpu.VMEM((positions, features), jnp.bfloat16),
        pltpu.VMEM(weight.shape, jnp.bfloat16),
        pltpu.VMEM((4, 3 * group, positions), F32),
        pltpu.VMEM((3, 3 * group, positions), F32),
        pltpu.VMEM((devices, share, block), F32),
        pltpu.VMEM((group, tile_rows, LANES), F32),
        pltpu.VMEM((n_seq, share, tile_rows, LANES), F32),
        pltpu.VMEM((group, tile_rows, LANES), F32),
        pltpu.VMEM((n_seq, share, tile_rows, LANES), F32),
        pltpu.VMEM((n_seq, share, tile_rows, LANES), F32),
        pltpu.VMEM((n_chan, group, block), jnp.bfloat16),
        pltpu.VMEM((n_chan, group, block), jnp.bfloat16),
        pltpu.VMEM((n1, share * LANES), F32),
        pltpu.VMEM((n1, share * LANES), F32),
        pltpu.VMEM((share * k_rows, 2 * LANES), F32),
        pltpu.VMEM((share * k_rows, 2 * LANES), F32),
        dma((total,)), dma((total,)), dma((total,)), dma((total,)), dma((3,)), dma((3,)),
        dma((devices,)), dma((devices,)), dma((n_seq,)), dma((n_seq,)), dma((n_seq,)),
        dma((n_seq,)), dma((n_chan,)), dma((n_chan,)), dma((1,)),
    ]
    out = pl.pallas_call(
        functools.partial(kernel, sizes),
        out_shape=jax.ShapeDtypeStruct((block, chan_width), jnp.bfloat16),
        in_specs=[hbm, hbm, hbm, vmem, vmem, vmem, vmem, vmem],
        out_specs=vmem,
        scratch_shapes=scratch,
        compiler_params=pltpu.CompilerParams(
            collective_id=0, has_side_effects=True, vmem_limit_bytes=48 * 2**20
        ),
        cost_estimate=pl.CostEstimate(
            flops=2 * positions * features * 3 * chan_width,
            bytes_accessed=10 * 2**20, transcendentals=0,
        ),
    )(layer_rows[0], weight, taps, first, twist, forward, back, last)
    return out[None]


def solution(mesh):
    in_specs = (
        P("section", "seq", "chan"),
        P("section", "chan", None),
        P("section", ("seq", "chan"), None),
        P("section", None),
    )
    out_specs = P("section", ("seq", "chan"), None)
    call = functools.partial(
        body, mesh.shape["section"], mesh.shape["seq"], mesh.shape["chan"]
    )
    return jax.shard_map(call, mesh=mesh, in_specs=in_specs, out_specs=out_specs, check_vma=False)
```

time: 303 us -> 92.4 us (0.30)
  waiting for transfers between devices: 207 us -> 0 us
  Pallas kernels: 0 us -> 79.8 us
  matrix products: 28.4 us -> 0 us
  starting transfers between devices: 23.6 us -> 0 us
  blocking collectives: 16.7 us -> 0 us
  between operations: 13.6 us -> 0.11 us
  other arithmetic: 5.74 us -> 1.43 us
  local copies, waits for them, and re-layouts: 6.86 us -> 10.7 us
    ppermute x1 -> x0, waiting for transfers between devices: 90.8 us -> none  [from_behind(): return lax.ppermute(value, axis, pairs)]
    pallas_call x0 -> x1, Pallas kernels: none -> 79.8 us  [body(): pl.pallas_call(functools.partial(kernel, sizes), out_shape=jax.ShapeDtype...]
    all_to_all x3 -> x0, waiting for transfers between devices: 76.9 us -> none  [transpose_blocks(): lax.all_to_all(data, ('seq', 'chan'), split_axis=0, concat_axis=1, tiled=...]
    reduce_scatter x1 -> x0, waiting for transfers between devices: 39.6 us -> none  [body(): lax.psum_scatter(jnp.dot(picked, in_weight[0], preferred_element_type=jnp...]
    dot_general x13 -> x0, matrix products: 28.4 us -> none  [the longest x12 23.3 us: mix(): return jnp.einsum(form, table, data, precision=lax.Precision.HIGHEST)]
    all_to_all x3 -> x0, starting transfers between devices: 20.6 us -> none  [transpose_blocks(): lax.all_to_all(data, ('seq', 'chan'), split_axis=0, concat_axis=1, tiled=...]
    all_to_all x1 -> x0, blocking collectives: 16.7 us -> none  [transpose_blocks(): lax.all_to_all(data, ('seq', 'chan'), split_axis=0, concat_axis=1, tiled=...]
    unnamed x8 -> x16, local copies, waits for them, and re-layouts: 0.02 us -> 7.24 us
  transfers between devices with their start and end apart: 5 -> 0, of which waited for: 5 -> 0; matrix products, arithmetic and copies ran while one was open for 0% -> 0% of each run, Pallas kernels for 0% -> 0%
where the time goes in v1:
time: 92.4 us; the launch traced here: 92 us
  Pallas kernels  79.8 us (86%)
  local copies, waits for them, and re-layouts  10.7 us (12%)
  other arithmetic  1.43 us (2%)
    pallas_call x1, Pallas kernels, body(): pl.pallas_call(functools.partial(kernel, sizes), out_shape=jax.ShapeDtype...  79.8 us
    unnamed x16, local copies, waits for them, and re-layouts  7.24 us
    transpose x1, local copies, waits for them, and re-layouts, body(): in_weight[0].reshape(features, 3, n_chan, group).transpose(2, 1, 3, 0)  2.33 us

profile of v1, /device:TPU:0, one launch (start us, length us, event | category | flops | bytes accessed | tf_op | source)
XLA Modules:
  0.0 92.0 jit_solution(12279567783459648075)
XLA Ops:
  0.0 4.7 %copy.12 = bf16[1,2048,768]{1,2,0:T(8,128)(2,1)} copy(bf16[1,2048,768]{2,1,0:T(8,128)(2,1)} %param.10) | data formatting | bytes 6291456 | tf_op args[1]
  4.7 0.0 copy-start.5
  4.7 0.0 copy-start.6
  4.7 0.0 copy-start.2
  4.7 0.0 copy-start.3
  4.7 0.0 copy-start.4
  4.7 2.3 %copy.13 = bf16[4,3,64,2048]{3,2,1,0:T(8,128)(2,1)S(1)} copy(bf16[4,3,64,2048]{3,2,0,1:T(8,128)(2,1)} %bitcast.16) | data formatting | bytes 6291456 | tf_op jit(solution)/shard_map/transpose | solution.py:334
  7.0 0.0 copy-done.5
  7.1 0.0 copy-done.6
  7.1 0.7 fusion
  7.8 0.7 maximum_bitcast_fusion
  8.5 1.1 %copy.14 = f32[256,256]{1,0:T(8,128)S(1)} copy(f32[256,256]{0,1:T(8,128)} %maximum_bitcast_fusion) | data formatting | bytes 524288 | tf_op jit(solution)/shard_map/transpose | solution.py:340
  9.6 0.0 copy-done.2
  9.6 0.0 copy-done.3
  9.6 0.0 copy-done.4
  9.6 0.0 copy-start
  9.6 0.9 %copy-done = f32[256,256]{1,0:T(8,128)S(1)} copy-done((f32[256,256]{1,0:T(8,128)S(1)}, f32[256,256]{1,0:T(8,128)}, u32[]{:S(2)}) %copy-start) | copy-done | bytes 262168
  10.6 0.0 copy-start.1
  10.6 0.9 %copy-done.1 = f32[256,256]{1,0:T(8,128)S(1)} copy-done((f32[256,256]{1,0:T(8,128)S(1)}, f32[256,256]{1,0:T(8,128)}, u32[]{:S(2)}) %copy-start.1) | copy-done | bytes 262168
  11.5 79.8 %shard_map.91 = bf16[256,256]{1,0:T(8,128)(2,1)S(1)} custom-call(bf16[1024,2048]{1,0:T(8,128)(2,1)} %bitcast.17, bf16[16,48,2048]{2,1,0:T(8,128)(2,1)S(1)} %bitcast.13, f32[16,16,256]{2,1,0:T(8,128)S(1)} %bitcast.14, f32[80,32]{1,0:T(8,128)S(1)} %copy-done.2, f32[2,40,128]{2,1,0:T(8,128)S(1)} %copy-done.3, f32[256,256]{1,0:T(8,128)S(1)} %copy-done, ...), custom_call_target="tpu_custom_call" | custom-call | flops 3221225472 | bytes 10485760 | tf_op jit(solution)/shard_map/pallas_call | solution.py:368
  91.4 0.7 copy.16
  (1 shorter events, 0.0 us)
Async XLA Ops:
  4.7 2.4 %copy-start.5 = (f32[1,256,256]{2,1,0:T(8,128)S(1)}, f32[1,256,256]{2,1,0:T(8,128)}, u32[]{:S(2)}) copy-start(f32[1,256,256]{2,1,0:T(8,128)} %param.11) | copy-start | bytes 786436
  4.7 2.4 %copy-start.6 = (f32[1,256]{1,0:T(1,128)S(1)}, f32[1,256]{1,0:T(1,128)}, u32[]{:S(2)}) copy-start(f32[1,256]{1,0:T(1,128)} %param.12) | copy-start | bytes 3076
  4.7 4.9 %copy-start.2 = (f32[80,32]{1,0:T(8,128)S(1)}, f32[80,32]{1,0:T(8,128)}, u32[]{:S(2)}) copy-start(f32[80,32]{1,0:T(8,128)} %constant.23.clone.first_ref) | copy-start | bytes 30724
  4.7 4.9 %copy-start.3 = (f32[2,40,128]{2,1,0:T(8,128)S(1)}, f32[2,40,128]{2,1,0:T(8,128)}, u32[]{:S(2)}) copy-start(f32[2,40,128]{2,1,0:T(8,128)} %constant.24.clone.twist_ref) | copy-start | bytes 122884
  4.7 4.9 %copy-start.4 = (f32[32,80]{1,0:T(8,128)S(1)}, f32[32,80]{1,0:T(8,128)}, u32[]{:S(2)}) copy-start(f32[32,80]{1,0:T(8,128)} %constant.27.clone.last_ref) | copy-start | bytes 30724
  9.6 1.0 %copy-start = (f32[256,256]{1,0:T(8,128)S(1)}, f32[256,256]{1,0:T(8,128)}, u32[]{:S(2)}) copy-start(f32[256,256]{1,0:T(8,128)} %constant.25.clone.forward_ref) | copy-start | bytes 786436
  10.6 0.9 %copy-start.1 = (f32[256,256]{1,0:T(8,128)S(1)}, f32[256,256]{1,0:T(8,128)}, u32[]{:S(2)}) copy-start(f32[256,256]{1,0:T(8,128)} %constant.26.clone.back_ref) | copy-start | bytes 786436

commit v2 on v1

--- a/solution.py
+++ b/solution.py
@@ -11,6 +11,8 @@
 
 LANES = 128
 PIECES = 2
+BLOCKS = 6
+AHEAD = 4
 MESH = pl.DeviceIdType.MESH
 F32 = jnp.float32
 
@@ -40,16 +42,24 @@
     return first, twist, forward, back, last
 
 
+def parts_of(a):
+    high = a.astype(jnp.bfloat16)
+    return high, (a - high.astype(F32)).astype(jnp.bfloat16)
+
+
 def exact(a, b):
-    return jnp.dot(a, b, precision=lax.Precision.HIGHEST, preferred_element_type=F32)
+    a_high, a_low = parts_of(a)
+    b_high, b_low = parts_of(b)
+    dot = functools.partial(jnp.dot, preferred_element_type=F32)
+    return dot(a_high, b_high) + (dot(a_high, b_low) + dot(a_low, b_high))
 
 
 def kernel(
     sizes,
     rows_hbm, weight_hbm, filter_hbm, first_ref, twist_ref, forward_ref, back_ref, last_ref,
     out_ref,
-    rows_v, wbuf, part, held, fil_in, sig_out, sig_in, query, conv_out, conv_in, gate_out, gate_in,
-    fil_line, line, spec_in, fil_spec,
+    rows_v, wbuf, part, held, crossed, fil_in, sig_out, sig_in, query, conv_out, conv_in, gate_out, gate_in,
+    stack, line, spec_in, fil_spec, sig_spec,
     y_send, y_recv, z_send, z_recv, r_send, r_recv, f_send, f_recv,
     a_send, a_recv, b_send, b_recv, o_send, o_recv, local_sem,
 ):
@@ -61,8 +71,8 @@
     mate = z + 1 - 2 * half
     c1 = c + 1 - 2 * lax.rem(c, 2)
     c2 = lax.rem(c + 2, 4)
-    c3 = 3 - c
-    order = (c3, c2, c1, c)
+    own = lax.rem(c, 2)
+    other_side, own_side = 1 - c // 2, c // 2
 
     def place(s, seq, chan):
         return (s, seq, chan)
@@ -118,35 +128,44 @@
         filter_wait(i).wait_recv()
         return carry
 
-    total = 4 * PIECES
-
-    def piece(k, which):
-        return order[k // PIECES] * (2 * PIECES) + which * PIECES + k % PIECES
+    total = BLOCKS * PIECES
+    positions, features = rows_v.shape
+    depth = features // (2 * PIECES)
+    pair = 2 * group
+
+    def block_of(j):
+        return (j % 3) * 2 + (other_side if j < 3 else own_side)
 
     def over_y(k):
-        at = piece(k, half)
-        return remote(
-            weight_hbm.at[at], wbuf.at[at], y_send.at[k], y_recv.at[k], place(behind, z, c)
+        block, at = block_of(k // PIECES), half * PIECES + k % PIECES
+        source = weight_hbm.at[
+            pl.ds(pl.multiple_of(at * depth, depth), depth),
+            pl.ds(pl.multiple_of(block * pair, pair), pair),
+        ]
+        return remote(
+            source, wbuf.at[block, at], y_send.at[k], y_recv.at[k], place(behind, z, c)
         )
 
     def over_z(k):
-        at = piece(k, half)
-        return remote(wbuf.at[at], wbuf.at[at], z_send.at[k], z_recv.at[k], place(sec, mate, c))
+        block, at = block_of(k // PIECES), half * PIECES + k % PIECES
+        held_piece = wbuf.at[block, at]
+        return remote(held_piece, held_piece, z_send.at[k], z_recv.at[k], place(sec, mate, c))
 
     def from_z(k):
-        at = piece(k, 1 - half)
-        return remote(wbuf.at[at], wbuf.at[at], z_send.at[k], z_recv.at[k], place(sec, mate, c))
-
-    positions = rows_v.shape[0]
-    columns = 3 * group
+        block, at = block_of(k // PIECES), (1 - half) * PIECES + k % PIECES
+        held_piece = wbuf.at[block, at]
+        return remote(held_piece, held_piece, z_send.at[k], z_recv.at[k], place(sec, mate, c))
+
     pos_tile = 256
-
-    def multiply(j, slot):
-        block = wbuf[pl.ds(order[j] * 2 * PIECES, 2 * PIECES)].reshape(columns, rows_v.shape[1])
+    own_rows = pl.ds(pl.multiple_of(own * group, group), group)
+    pair_rows = pl.ds(pl.multiple_of((1 - own) * group, group), group)
+
+    def multiply(j):
+        block = wbuf[block_of(j)].reshape(features, pair).T
 
         def tile(t, carry):
             at = pl.multiple_of(t * pos_tile, pos_tile)
-            part[slot, :, pl.ds(at, pos_tile)] = lax.dot_general(
+            part[j, :, pl.ds(at, pos_tile)] = lax.dot_general(
                 block, rows_v[pl.ds(at, pos_tile), :], (((1,), (1,)), ((), ())),
                 preferred_element_type=F32,
             )
@@ -154,12 +173,21 @@
 
         lax.fori_loop(0, positions // pos_tile, tile, 0)
 
-    to_pair = remote(part.at[0], held.at[0], r_send.at[0], r_recv.at[0], place(sec, z, c1))
-    to_cross = remote(part.at[1], held.at[1], r_send.at[1], r_recv.at[1], place(sec, z, c2))
-    to_pair_last = remote(part.at[2], held.at[2], r_send.at[2], r_recv.at[2], place(sec, z, c1))
-
-    def spectrum(source, target):
-        mixed = exact(first_ref[...], source[...])
+    def to_pair(j):
+        return remote(
+            part.at[j, pair_rows], held.at[j], r_send.at[j], r_recv.at[j], place(sec, z, c1)
+        )
+
+    def to_cross(j):
+        return remote(
+            part.at[j, own_rows], crossed.at[j], r_send.at[BLOCKS + j], r_recv.at[BLOCKS + j],
+            place(sec, z, c2),
+        )
+
+    def spectrum(target):
+        for a in range(share):
+            line[:, a * LANES : (a + 1) * LANES] = stack[a]
+        mixed = exact(first_ref[...], line[...])
         for a in range(share):
             lanes = slice(a * LANES, (a + 1) * LANES)
             real, imag = mixed[:k_rows, lanes], mixed[k_rows:, lanes]
@@ -171,78 +199,71 @@
     def process(j):
         for k in range(j * PIECES, (j + 1) * PIECES):
             from_z(k).wait_recv()
-        multiply(j, j)
-        if j == 0:
-            to_pair.start()
-        if j == 1:
-            to_pair.wait_recv()
-            part[1] = part[1] + held[0]
-            to_cross.start()
-        if j == 2:
-            to_pair_last.start()
-
-    over_y(0).start()
-    over_y(1).start()
+        multiply(j)
+        to_pair(j).start()
+        if 1 <= j <= 3:
+            to_pair(j - 1).wait_recv()
+            part[j - 1, own_rows] = part[j - 1, own_rows] + held[j - 1]
+            to_cross(j - 1).start()
+
     lax.fori_loop(0, n_seq * n_chan, start_filter, 0)
+    for k in range(AHEAD):
+        over_y(k).start()
     rows_copy.wait()
     for k in range(total):
         over_y(k).wait_recv()
         over_z(k).start()
         over_y(k).wait_send()
-        if k + 2 < total:
-            over_y(k + 2).start()
-        if k == PIECES:
+        if k + AHEAD < total:
+            over_y(k + AHEAD).start()
+        if k == 2 * PIECES:
             lax.fori_loop(0, n_seq * n_chan, end_filter, 0)
             per = fil_in.shape[2] // LANES
             for i in range(n_seq * n_chan):
+                block = fil_in[i].astype(F32)
                 for r in range(per):
-                    for a in range(share):
-                        fil_line[i * per + r : i * per + r + 1, a * LANES : (a + 1) * LANES] = (
-                            fil_in[i, a : a + 1, r * LANES : (r + 1) * LANES]
-                        )
-            spectrum(fil_line, fil_spec)
+                    stack[:, i * per + r, :] = block[:, r * LANES : (r + 1) * LANES]
+            spectrum(fil_spec)
         if k % PIECES == PIECES - 1 and k >= PIECES:
             process(k // PIECES - 1)
-    process(3)
-    to_pair_last.wait_recv()
-    to_cross.wait_recv()
-    mixed = (part[3] + held[2] + held[1]).astype(jnp.bfloat16).astype(F32)
-    signal = mixed[group : 2 * group] * mixed[2 * group :]
-    for r in range(tile_rows):
-        lanes = slice(r * LANES, (r + 1) * LANES)
-        sig_out[:, r, :] = signal[:, lanes]
-        query[:, r, :] = mixed[:group, lanes]
+    process(BLOCKS - 1)
+    gathered = []
+    for t in range(3):
+        to_cross(t).wait_recv()
+        to_pair(3 + t).wait_recv()
+        total_part = part[3 + t, own_rows] + held[3 + t] + crossed[t]
+        gathered.append(total_part.astype(jnp.bfloat16).astype(F32))
+    query[...] = gathered[0]
+    signal = gathered[1] * gathered[2]
+    for i in range(n_seq):
+        sig_out[i] = signal[i * share : (i + 1) * share].astype(jnp.bfloat16)
 
     def sig_copy(step):
         to = lax.rem(z + step, n_seq)
         return remote(
-            sig_out.at[pl.ds(to * share, share)], sig_in.at[z], a_send.at[step], a_recv.at[step],
+            sig_out.at[to], sig_in.at[z], a_send.at[step], a_recv.at[step],
             place(sec, to, c),
         )
 
     def sig_wait(step):
         source = lax.rem(z + n_seq - step, n_seq)
         return remote(
-            sig_out.at[pl.ds(0, share)], sig_in.at[source], a_send.at[step], a_recv.at[step],
+            sig_out.at[0], sig_in.at[source], a_send.at[step], a_recv.at[step],
             place(sec, source, c),
         )
 
     for step in range(1, n_seq):
         sig_copy(step).start()
-    sig_in[z] = sig_out[pl.ds(z * share, share)]
+    sig_in[z] = sig_out[z]
     for step in range(1, n_seq):
         sig_wait(step).wait_recv()
 
-    for a in range(share):
-        line[:, a * LANES : (a + 1) * LANES] = sig_in[:, a].reshape(n_seq * tile_rows, LANES)
-    mixed_first = exact(first_ref[...], line[...])
-    for a in range(share):
-        lanes = slice(a * LANES, (a + 1) * LANES)
-        real, imag = mixed_first[:k_rows, lanes], mixed_first[k_rows:, lanes]
-        span = slice(a * k_rows, (a + 1) * k_rows)
-        spec_in[span, :LANES] = real * twist_ref[0] + imag * twist_ref[1]
-        spec_in[span, LANES:] = imag * twist_ref[0] - real * twist_ref[1]
-    spec = exact(spec_in[...], forward_ref[...])
+    for i in range(n_seq):
+        block = sig_in[i].astype(F32)
+        for r in range(tile_rows):
+            stack[:, i * tile_rows + r, :] = block[:, r * LANES : (r + 1) * LANES]
+    spectrum(sig_spec)
+    spec = sig_spec[...]
     sr, si = spec[:, :LANES], spec[:, LANES:]
     fr, fi = fil_spec[:, :LANES], fil_spec[:, LANES:]
     spec_in[:, :LANES] = sr * fr - si * fi
@@ -263,7 +284,12 @@
         )
     conv = exact(last_ref[...], jnp.concatenate(turned, axis=1))
     for a in range(share):
-        conv_out[:, a] = conv[:, a * LANES : (a + 1) * LANES].reshape(n_seq, tile_rows, LANES)
+        stack[a] = conv[:, a * LANES : (a + 1) * LANES]
+    for i in range(n_seq):
+        for r in range(tile_rows):
+            conv_out[i, :, r * LANES : (r + 1) * LANES] = stack[:, i * tile_rows + r, :].astype(
+                jnp.bfloat16
+            )
 
     def conv_copy(step):
         to = lax.rem(z + step, n_seq)
@@ -285,11 +311,9 @@
         conv_wait(step).wait_recv()
 
     per = tile_rows // n_chan
-    for r in range(tile_rows):
-        gated = query[:, r, :] * conv_in[:, :, r, :].reshape(group, LANES)
-        gate_out[r // per, :, (r % per) * LANES : (r % per + 1) * LANES] = gated.astype(
-            jnp.bfloat16
-        )
+    gated = query[...] * conv_in[...].astype(F32).reshape(group, positions)
+    for to in range(n_chan):
+        gate_out[to] = gated[:, to * per * LANES : (to + 1) * per * LANES].astype(jnp.bfloat16)
 
     def gate_copy(to):
         return remote(
@@ -311,9 +335,10 @@
 
     for k in range(total):
         over_z(k).wait_send()
-    to_pair.wait_send()
-    to_cross.wait_send()
-    to_pair_last.wait_send()
+    for j in range(BLOCKS):
+        to_pair(j).wait_send()
+    for j in range(3):
+        to_cross(j).wait_send()
     for step in range(1, n_seq):
         sig_copy(step).wait_send()
         conv_copy(step).wait_send()
@@ -331,37 +356,39 @@
     n1 = n_seq * tile_rows
     first, twist, forward, back, last = tables(n_seq * positions)
     k_rows = twist.shape[1]
-    weight = in_weight[0].reshape(features, 3, n_chan, group).transpose(2, 1, 3, 0)
-    width = 3 * group // (2 * PIECES)
-    weight = weight.reshape(n_chan * 2 * PIECES, width, features)
+    weight = in_weight[0]
+    pair = 2 * group
     at_start = lax.axis_index(("seq", "chan")) == 0
     tap = jnp.where(at_start, skip_gain[0], 0.0)
     taps = jnp.concatenate([long_filter[0, :1] + tap[None, :], long_filter[0, 1:]], axis=0)
-    taps = taps.T.reshape(n_chan * n_seq, share, block)
+    taps = taps.astype(jnp.bfloat16).T.reshape(n_chan * n_seq, share, block)
     sizes = (n_sec, n_seq, n_chan, group, share, tile_rows, k_rows)
     vmem = pl.BlockSpec(memory_space=pltpu.VMEM)
     hbm = pl.BlockSpec(memory_space=pl.ANY)
     dma = pltpu.SemaphoreType.DMA
     devices = n_seq * n_chan
-    total = 4 * PIECES
+    total = BLOCKS * PIECES
     scratch = [
         pltpu.VMEM((positions, features), jnp.bfloat16),
-        pltpu.VMEM(weight.shape, jnp.bfloat16),
-        pltpu.VMEM((4, 3 * group, positions), F32),
-        pltpu.VMEM((3, 3 * group, positions), F32),
-        pltpu.VMEM((devices, share, block), F32),
-        pltpu.VMEM((group, tile_rows, LANES), F32),
-        pltpu.VMEM((n_seq, share, tile_rows, LANES), F32),
-        pltpu.VMEM((group, tile_rows, LANES), F32),
-        pltpu.VMEM((n_seq, share, tile_rows, LANES), F32),
-        pltpu.VMEM((n_seq, share, tile_rows, LANES), F32),
+        pltpu.VMEM((BLOCKS, 2 * PIECES, features // (2 * PIECES), pair), jnp.bfloat16),
+        pltpu.VMEM((BLOCKS, pair, positions), F32),
+        pltpu.VMEM((BLOCKS, group, positions), F32),
+        pltpu.VMEM((3, group, positions), F32),
+        pltpu.VMEM((devices, share, block), jnp.bfloat16),
+        pltpu.VMEM((n_seq, share, positions), jnp.bfloat16),
+        pltpu.VMEM((n_seq, share, positions), jnp.bfloat16),
+        pltpu.VMEM((group, positions), F32),
+        pltpu.VMEM((n_seq, share, positions), jnp.bfloat16),
+        pltpu.VMEM((n_seq, share, positions), jnp.bfloat16),
         pltpu.VMEM((n_chan, group, block), jnp.bfloat16),
         pltpu.VMEM((n_chan, group, block), jnp.bfloat16),
-        pltpu.VMEM((n1, share * LANES), F32),
+        pltpu.VMEM((share, n1, LANES), F32),
         pltpu.VMEM((n1, share * LANES), F32),
         pltpu.VMEM((share * k_rows, 2 * LANES), F32),
         pltpu.VMEM((share * k_rows, 2 * LANES), F32),
-        dma((total,)), dma((total,)), dma((total,)), dma((total,)), dma((3,)), dma((3,)),
+        pltpu.VMEM((share * k_rows, 2 * LANES), F32),
+        dma((total,)), dma((total,)), dma((total,)), dma((total,)), dma((BLOCKS + 3,)),
+        dma((BLOCKS + 3,)),
         dma((devices,)), dma((devices,)), dma((n_seq,)), dma((n_seq,)), dma((n_seq,)),
         dma((n_seq,)), dma((n_chan,)), dma((n_chan,)), dma((1,)),
     ]

time: 92.4 us -> 77.7 us (0.84)
  Pallas kernels: 79.8 us -> 68.7 us
  local copies, waits for them, and re-layouts: 10.7 us -> 7.79 us
    pallas_call x1, Pallas kernels: 79.8 us -> 68.7 us  [body(): pl.pallas_call(functools.partial(kernel, sizes), out_shape=jax.ShapeDtype...]
    transpose x2 -> x1, local copies, waits for them, and re-layouts: 3.41 us -> 0.1 us  [body(): taps = taps.astype(jnp.bfloat16).T.reshape(n_chan * n_seq, share, block)]
    squeeze x1, local copies, waits for them, and re-layouts: 0.02 us -> 0.97 us  [body(): long_filter[0, 1:]]
    unnamed x16 -> x13, local copies, waits for them, and re-layouts: 7.24 us -> 6.71 us
where the time goes in v2:
time: 77.7 us; the launch traced here: 77.3 us
  Pallas kernels  68.7 us (88%)
  local copies, waits for them, and re-layouts  7.79 us (10%)
    pallas_call x1, Pallas kernels, body(): pl.pallas_call(functools.partial(kernel, sizes), out_shape=jax.ShapeDtype...  68.7 us
    unnamed x13, local copies, waits for them, and re-layouts  6.71 us

profile of v2, /device:TPU:0, one launch (start us, length us, event | category | flops | bytes accessed | tf_op | source)
XLA Modules:
  0.0 77.3 jit_solution(9664429245628777074)
XLA Ops:
  0.0 0.7 fusion.2
  0.7 1.0 %fusion = bf16[255,256]{1,0:T(8,128)(2,1)S(1)} fusion(f32[1,256,256]{2,1,0:T(8,128)} %param.11), kind=kLoop, calls=%fused_computation.1 | loop fusion | bytes 261120 | tf_op jit(solution)/shard_map/squeeze | solution.py:363
  1.7 0.1 copy.10
  1.8 0.0 copy-start
  1.9 1.9 %copy-done = bf16[1,2048,768]{2,1,0:T(8,128)(2,1)S(1)} copy-done((bf16[1,2048,768]{2,1,0:T(8,128)(2,1)S(1)}, bf16[1,2048,768]{2,1,0:T(8,128)(2,1)}, u32[]{:S(2)}) %copy-start) | copy-done | bytes 3145752
  3.7 0.0 copy-start.1
  3.7 0.9 %copy-done.1 = f32[256,256]{1,0:T(8,128)S(1)} copy-done((f32[256,256]{1,0:T(8,128)S(1)}, f32[256,256]{1,0:T(8,128)}, u32[]{:S(2)}) %copy-start.1) | copy-done | bytes 262168
  4.7 0.0 copy-start.2
  4.7 0.9 %copy-done.2 = f32[256,256]{1,0:T(8,128)S(1)} copy-done((f32[256,256]{1,0:T(8,128)S(1)}, f32[256,256]{1,0:T(8,128)}, u32[]{:S(2)}) %copy-start.2) | copy-done | bytes 262168
  5.6 0.0 copy-start.3
  5.6 0.8 %copy-done.3 = f32[2,40,128]{2,1,0:T(8,128)S(1)} copy-done((f32[2,40,128]{2,1,0:T(8,128)S(1)}, f32[2,40,128]{2,1,0:T(8,128)}, u32[]{:S(2)}) %copy-start.3) | copy-done | bytes 40984
  6.4 0.0 copy-start.4
  6.4 0.8 %copy-done.4 = f32[80,32]{1,0:T(8,128)S(1)} copy-done((f32[80,32]{1,0:T(8,128)S(1)}, f32[80,32]{1,0:T(8,128)}, u32[]{:S(2)}) %copy-start.4) | copy-done | bytes 10264
  7.2 0.0 copy-start.5
  7.2 0.7 copy-done.5
  7.9 68.7 %shard_map.91 = bf16[256,256]{1,0:T(8,128)(2,1)S(1)} custom-call(bf16[1024,2048]{1,0:T(8,128)(2,1)} %bitcast.13, bf16[2048,768]{1,0:T(8,128)(2,1)S(1)} %bitcast.12, bf16[16,16,256]{2,1,0:T(8,128)(2,1)S(1)} %bitcast.10, f32[80,32]{1,0:T(8,128)S(1)} %copy-done.4, f32[2,40,128]{2,1,0:T(8,128)S(1)} %copy-done.3, f32[256,256]{1,0:T(8,128)S(1)} %copy-done.2, ...), custom_call_target="tpu_custom_call" | custom-call | flops 3221225472 | bytes 10485760 | tf_op jit(solution)/shard_map/pallas_call | solution.py:395
  76.6 0.7 copy.12
  (1 shorter events, 0.0 us)
Async XLA Ops:
  1.8 1.9 %copy-start = (bf16[1,2048,768]{2,1,0:T(8,128)(2,1)S(1)}, bf16[1,2048,768]{2,1,0:T(8,128)(2,1)}, u32[]{:S(2)}) copy-start(bf16[1,2048,768]{2,1,0:T(8,128)(2,1)} %param.10) | copy-start | bytes 9437188
  3.7 0.9 %copy-start.1 = (f32[256,256]{1,0:T(8,128)S(1)}, f32[256,256]{1,0:T(8,128)}, u32[]{:S(2)}) copy-start(f32[256,256]{1,0:T(8,128)} %constant.26.clone.back_ref) | copy-start | bytes 786436
  4.7 0.9 %copy-start.2 = (f32[256,256]{1,0:T(8,128)S(1)}, f32[256,256]{1,0:T(8,128)}, u32[]{:S(2)}) copy-start(f32[256,256]{1,0:T(8,128)} %constant.25.clone.forward_ref) | copy-start | bytes 786436
  5.6 0.8 %copy-start.3 = (f32[2,40,128]{2,1,0:T(8,128)S(1)}, f32[2,40,128]{2,1,0:T(8,128)}, u32[]{:S(2)}) copy-start(f32[2,40,128]{2,1,0:T(8,128)} %constant.24.clone.twist_ref) | copy-start | bytes 122884
  6.4 0.8 %copy-start.4 = (f32[80,32]{1,0:T(8,128)S(1)}, f32[80,32]{1,0:T(8,128)}, u32[]{:S(2)}) copy-start(f32[80,32]{1,0:T(8,128)} %constant.23.clone.first_ref) | copy-start | bytes 30724
  7.2 0.7 copy-start.5

commit v3 on v2

--- a/solution.py
+++ b/solution.py
@@ -42,6 +42,12 @@
     return first, twist, forward, back, last
 
 
+def packed_tables(positions):
+    first, twist, forward, back, last = tables(positions)
+    wide = [forward, back, np.concatenate([twist[0], twist[1]], axis=1), first, last]
+    return np.concatenate([np.pad(t, ((0, 0), (0, 2 * LANES - t.shape[1]))) for t in wide])
+
+
 def parts_of(a):
     high = a.astype(jnp.bfloat16)
     return high, (a - high.astype(F32)).astype(jnp.bfloat16)
@@ -56,9 +62,9 @@
 
 def kernel(
     sizes,
-    rows_hbm, weight_hbm, filter_hbm, first_ref, twist_ref, forward_ref, back_ref, last_ref,
+    rows_hbm, weight_hbm, filter_hbm, table_hbm,
     out_ref,
-    rows_v, wbuf, part, held, crossed, fil_in, sig_out, sig_in, query, conv_out, conv_in, gate_out, gate_in,
+    table, rows_v, wbuf, part, held, crossed, fil_in, sig_out, sig_in, query, conv_out, conv_in, gate_out, gate_in,
     stack, line, spec_in, fil_spec, sig_spec,
     y_send, y_recv, z_send, z_recv, r_send, r_recv, f_send, f_recv,
     a_send, a_recv, b_send, b_recv, o_send, o_recv, local_sem,
@@ -79,6 +85,17 @@
 
     rows_copy = pltpu.make_async_copy(rows_hbm, rows_v, local_sem.at[0])
     rows_copy.start()
+    table_copy = pltpu.make_async_copy(table_hbm, table, local_sem.at[1])
+    table_copy.start()
+    n1 = table.shape[0] - 4 * LANES - 3 * k_rows
+    forward_ref = table.at[: 2 * LANES]
+    back_ref = table.at[2 * LANES : 4 * LANES]
+    twist_ref = [
+        table.at[4 * LANES : 4 * LANES + k_rows, :LANES],
+        table.at[4 * LANES : 4 * LANES + k_rows, LANES:],
+    ]
+    first_ref = table.at[4 * LANES + k_rows : 4 * LANES + 3 * k_rows, :n1]
+    last_ref = table.at[4 * LANES + 3 * k_rows :, : 2 * k_rows]
 
     barrier = pltpu.get_barrier_semaphore()
 
@@ -156,19 +173,18 @@
         held_piece = wbuf.at[block, at]
         return remote(held_piece, held_piece, z_send.at[k], z_recv.at[k], place(sec, mate, c))
 
-    pos_tile = 256
+    pos_tile = 512
     own_rows = pl.ds(pl.multiple_of(own * group, group), group)
     pair_rows = pl.ds(pl.multiple_of((1 - own) * group, group), group)
 
     def multiply(j):
-        block = wbuf[block_of(j)].reshape(features, pair).T
+        block = wbuf[block_of(j)].reshape(features, pair)
 
         def tile(t, carry):
             at = pl.multiple_of(t * pos_tile, pos_tile)
-            part[j, :, pl.ds(at, pos_tile)] = lax.dot_general(
-                block, rows_v[pl.ds(at, pos_tile), :], (((1,), (1,)), ((), ())),
-                preferred_element_type=F32,
-            )
+            part[j, :, pl.ds(at, pos_tile)] = jnp.dot(
+                rows_v[pl.ds(at, pos_tile), :], block, preferred_element_type=F32
+            ).T
             return carry
 
         lax.fori_loop(0, positions // pos_tile, tile, 0)
@@ -192,8 +208,8 @@
             lanes = slice(a * LANES, (a + 1) * LANES)
             real, imag = mixed[:k_rows, lanes], mixed[k_rows:, lanes]
             span = slice(a * k_rows, (a + 1) * k_rows)
-            spec_in[span, :LANES] = real * twist_ref[0] + imag * twist_ref[1]
-            spec_in[span, LANES:] = imag * twist_ref[0] - real * twist_ref[1]
+            spec_in[span, :LANES] = real * twist_ref[0][...] + imag * twist_ref[1][...]
+            spec_in[span, LANES:] = imag * twist_ref[0][...] - real * twist_ref[1][...]
         target[...] = exact(spec_in[...], forward_ref[...])
 
     def process(j):
@@ -210,20 +226,13 @@
     for k in range(AHEAD):
         over_y(k).start()
     rows_copy.wait()
+    table_copy.wait()
     for k in range(total):
         over_y(k).wait_recv()
         over_z(k).start()
         over_y(k).wait_send()
         if k + AHEAD < total:
             over_y(k + AHEAD).start()
-        if k == 2 * PIECES:
-            lax.fori_loop(0, n_seq * n_chan, end_filter, 0)
-            per = fil_in.shape[2] // LANES
-            for i in range(n_seq * n_chan):
-                block = fil_in[i].astype(F32)
-                for r in range(per):
-                    stack[:, i * per + r, :] = block[:, r * LANES : (r + 1) * LANES]
-            spectrum(fil_spec)
         if k % PIECES == PIECES - 1 and k >= PIECES:
             process(k // PIECES - 1)
     process(BLOCKS - 1)
@@ -255,6 +264,13 @@
     for step in range(1, n_seq):
         sig_copy(step).start()
     sig_in[z] = sig_out[z]
+    lax.fori_loop(0, n_seq * n_chan, end_filter, 0)
+    per = fil_in.shape[2] // LANES
+    for i in range(n_seq * n_chan):
+        block = fil_in[i].astype(F32)
+        for r in range(per):
+            stack[:, i * per + r, :] = block[:, r * LANES : (r + 1) * LANES]
+    spectrum(fil_spec)
     for step in range(1, n_seq):
         sig_wait(step).wait_recv()
 
@@ -276,8 +292,8 @@
         turned.append(
             jnp.concatenate(
                 [
-                    real * twist_ref[0] - imag * twist_ref[1],
-                    imag * twist_ref[0] + real * twist_ref[1],
+                    real * twist_ref[0][...] - imag * twist_ref[1][...],
+                    imag * twist_ref[0][...] + real * twist_ref[1][...],
                 ],
                 axis=0,
             )
@@ -354,8 +370,8 @@
     share = group // n_seq
     tile_rows = positions // LANES
     n1 = n_seq * tile_rows
-    first, twist, forward, back, last = tables(n_seq * positions)
-    k_rows = twist.shape[1]
+    table = packed_tables(n_seq * positions)
+    k_rows = (table.shape[0] - 4 * LANES - n1) // 3
     weight = in_weight[0]
     pair = 2 * group
     at_start = lax.axis_index(("seq", "chan")) == 0
@@ -369,6 +385,7 @@
     devices = n_seq * n_chan
     total = BLOCKS * PIECES
     scratch = [
+        pltpu.VMEM(table.shape, F32),
         pltpu.VMEM((positions, features), jnp.bfloat16),
         pltpu.VMEM((BLOCKS, 2 * PIECES, features // (2 * PIECES), pair), jnp.bfloat16),
         pltpu.VMEM((BLOCKS, pair, positions), F32),
@@ -390,22 +407,22 @@
         dma((total,)), dma((total,)), dma((total,)), dma((total,)), dma((BLOCKS + 3,)),
         dma((BLOCKS + 3,)),
         dma((devices,)), dma((devices,)), dma((n_seq,)), dma((n_seq,)), dma((n_seq,)),
-        dma((n_seq,)), dma((n_chan,)), dma((n_chan,)), dma((1,)),
+        dma((n_seq,)), dma((n_chan,)), dma((n_chan,)), dma((2,)),
     ]
     out = pl.pallas_call(
         functools.partial(kernel, sizes),
         out_shape=jax.ShapeDtypeStruct((block, chan_width), jnp.bfloat16),
-        in_specs=[hbm, hbm, hbm, vmem, vmem, vmem, vmem, vmem],
+        in_specs=[hbm, hbm, hbm, hbm],
         out_specs=vmem,
         scratch_shapes=scratch,
         compiler_params=pltpu.CompilerParams(
-            collective_id=0, has_side_effects=True, vmem_limit_bytes=48 * 2**20
+            collective_id=0, has_side_effects=True, vmem_limit_bytes=60 * 2**20
         ),
         cost_estimate=pl.CostEstimate(
             flops=2 * positions * features * 3 * chan_width,
             bytes_accessed=10 * 2**20, transcendentals=0,
         ),
-    )(layer_rows[0], weight, taps, first, twist, forward, back, last)
+    )(layer_rows[0], weight, taps, table)
     return out[None]
 
 

time: 77.7 us -> 73.5 us (0.946)
  local copies, waits for them, and re-layouts: 7.79 us -> 3.3 us
    unnamed x13 -> x1, local copies, waits for them, and re-layouts: 6.71 us -> 1.57 us
where the time goes in v3:
time: 73.5 us; the launch traced here: 73.2 us
  Pallas kernels  69.2 us (94%)
  local copies, waits for them, and re-layouts  3.3 us (4%)
  other arithmetic  0.75 us (1%)
    pallas_call x1, Pallas kernels, body(): pl.pallas_call(functools.partial(kernel, sizes), out_shape=jax.ShapeDtype...  69.2 us
    unnamed x1, local copies, waits for them, and re-layouts  1.57 us

profile of v3, /device:TPU:0, one launch (start us, length us, event | category | flops | bytes accessed | tf_op | source)
XLA Modules:
  0.0 73.2 jit_solution(1461869782740441055)
XLA Ops:
  0.0 0.7 fusion.2
  0.7 1.0 %fusion = bf16[255,256]{1,0:T(8,128)(2,1)S(1)} fusion(f32[1,256,256]{2,1,0:T(8,128)} %param.7), kind=kLoop, calls=%fused_computation.1 | loop fusion | bytes 261120 | tf_op jit(solution)/shard_map/squeeze | solution.py:379
  1.7 0.8 %copy.6 = bf16[256,256]{1,0:T(8,128)(2,1)} copy(bf16[256,256]{0,1:T(8,128)(2,1)S(1)} %maximum_bitcast_fusion) | data formatting | bytes 262144 | tf_op jit(solution)/shard_map/transpose | solution.py:380
  2.5 69.2 %shard_map.55 = bf16[256,256]{1,0:T(8,128)(2,1)} custom-call(bf16[1024,2048]{1,0:T(8,128)(2,1)} %bitcast.12, bf16[2048,768]{1,0:T(8,128)(2,1)} %bitcast.13, bf16[16,16,256]{2,1,0:T(8,128)(2,1)} %bitcast.10, f32[664,256]{1,0:T(8,128)} %constant.15.clone.table_hbm), custom_call_target="tpu_custom_call" | custom-call | flops 3221225472 | bytes 10485760 | tf_op jit(solution)/shard_map/pallas_call | solution.py:412
  71.7 1.6 %copy.8 = bf16[1,256,256]{2,1,0:T(8,128)(2,1)} copy(bf16[1,256,256]{2,1,0:T(8,128)(2,1)} %bitcast.11) | data formatting | bytes 262144
  (1 shorter events, 0.0 us)

commit v4 on v3

--- a/solution.py
+++ b/solution.py
@@ -12,7 +12,7 @@
 LANES = 128
 PIECES = 2
 BLOCKS = 6
-AHEAD = 4
+AHEAD = 2
 MESH = pl.DeviceIdType.MESH
 F32 = jnp.float32
 
@@ -222,7 +222,6 @@
             part[j - 1, own_rows] = part[j - 1, own_rows] + held[j - 1]
             to_cross(j - 1).start()
 
-    lax.fori_loop(0, n_seq * n_chan, start_filter, 0)
     for k in range(AHEAD):
         over_y(k).start()
     rows_copy.wait()
@@ -233,6 +232,8 @@
         over_y(k).wait_send()
         if k + AHEAD < total:
             over_y(k + AHEAD).start()
+        if k == total - AHEAD - 2:
+            lax.fori_loop(0, n_seq * n_chan, start_filter, 0)
         if k % PIECES == PIECES - 1 and k >= PIECES:
             process(k // PIECES - 1)
     process(BLOCKS - 1)

time: 73.5 us -> 73.1 us (level)
  no operation moved by 1% of the time
where the time goes in v4:
time: 73.1 us; the launch traced here: 72.9 us
  Pallas kernels  68.8 us (94%)
  local copies, waits for them, and re-layouts  3.3 us (5%)
  other arithmetic  0.75 us (1%)
    pallas_call x1, Pallas kernels, body(): pl.pallas_call(functools.partial(kernel, sizes), out_shape=jax.ShapeDtype...  68.8 us
    unnamed x1, local copies, waits for them, and re-layouts  1.57 us

profile of v4, /device:TPU:0, one launch (start us, length us, event | category | flops | bytes accessed | tf_op | source)
XLA Modules:
  0.0 72.9 jit_solution(4701230852280546864)
XLA Ops:
  0.0 0.7 fusion.2
  0.7 1.0 %fusion = bf16[255,256]{1,0:T(8,128)(2,1)S(1)} fusion(f32[1,256,256]{2,1,0:T(8,128)} %param.7), kind=kLoop, calls=%fused_computation.1 | loop fusion | bytes 261120 | tf_op jit(solution)/shard_map/squeeze | solution.py:380
  1.7 0.8 %copy.6 = bf16[256,256]{1,0:T(8,128)(2,1)} copy(bf16[256,256]{0,1:T(8,128)(2,1)S(1)} %maximum_bitcast_fusion) | data formatting | bytes 262144 | tf_op jit(solution)/shard_map/transpose | solution.py:381
  2.5 68.8 %shard_map.55 = bf16[256,256]{1,0:T(8,128)(2,1)} custom-call(bf16[1024,2048]{1,0:T(8,128)(2,1)} %bitcast.12, bf16[2048,768]{1,0:T(8,128)(2,1)} %bitcast.13, bf16[16,16,256]{2,1,0:T(8,128)(2,1)} %bitcast.10, f32[664,256]{1,0:T(8,128)} %constant.15.clone.table_hbm), custom_call_target="tpu_custom_call" | custom-call | flops 3221225472 | bytes 10485760 | tf_op jit(solution)/shard_map/pallas_call | solution.py:413
  71.4 1.6 %copy.8 = bf16[1,256,256]{2,1,0:T(8,128)(2,1)} copy(bf16[1,256,256]{2,1,0:T(8,128)(2,1)} %bitcast.11) | data formatting | bytes 262144
  (1 shorter events, 0.0 us)
